TPU v7x, 512 devices: a whole 4x8x8 slice. The times are simulated.
512 devices in a mesh: tm: 128 (over y, z, core), grp: 4 (over x).
Axes of the slice: x: 4, y: 8, z: 8, core: 2. Of those that a mesh axis runs over, the one named last changes fastest.
Arguments:
- recording: bfloat16 [384, 524288], P(None, ('tm', 'grp')), may hold values from -6 to 6
- spatial_maps: bfloat16 [64, 384], replicated, may hold values from -0.3125 to 0.3125
- temporal_atoms: float32 [64, 64], replicated, may hold values from -0.75 to 0.75
- codes_init: float32 [64, 524288], P(None, ('tm', 'grp')), may hold values from 0 to 1
- step_sizes: float32 [64], replicated, may hold values from 0.02 to 0.08
- thresholds: float32 [64], replicated, may hold values from 0.02 to 0.3
- active_ids: int32 [512, 16], P(('tm', 'grp')), may hold values from 0 to 63, as said below
- active_counts: int32 [512], P(('tm', 'grp')), may hold values from 1 to 16, as said below
- owner_slots: int32 [64], replicated, may hold values from 0 to 255, as said below
Outputs:
- new_codes: float32 [64, 524288], P(None, ('tm', 'grp'))
- owned_panels: float32 [1024, 24576], P(('tm', 'grp'))
Inputs may be any that keep to these rules, and one draw needn't show every extreme that they name: `active_ids`: the 16 atoms of one shard's list are distinct. `active_counts`: some shard's list is full. `owner_slots`: atoms of one block of 16 atoms (k // 16 equal) have distinct slots.
All inputs are finite; a program needn't handle non-finite values.
Results may differ from a plain program's by a relative error of at most 0.0034.
Values may be sent and summed in bfloat16 or wider, within the bound.
A program may use at most 64 MiB of HBM per device.

v0:
```python
import jax
import jax.numpy as jnp
from jax import lax
from jax.sharding import PartitionSpec as P

ITERS = 3
OWN = 2


PRECISE = lax.Precision.HIGHEST


def from_behind(array, axis, by):
    length = lax.axis_size(axis)
    pairs = [(i, i + by) for i in range(length) if 0 <= i + by < length]
    return lax.ppermute(array, axis, pairs)


def depthwise(signal, kernel):
    return lax.conv_general_dilated(
        signal[None],
        kernel[:, None, :],
        (1,),
        "VALID",
        feature_group_count=kernel.shape[0],
        precision=PRECISE,
    )[0]


def lagged(picked, tap_count):
    shard_len = picked.shape[1]
    padded = jnp.pad(picked, ((0, 0), (tap_count - 1, tap_count - 1)))
    return jnp.stack(
        [
            padded[:, tap_count - 1 - lag : tap_count - 1 - lag + shard_len + tap_count - 1]
            for lag in range(tap_count)
        ],
        axis=1,
    )


def body(
    recording,
    spatial_maps,
    temporal_atoms,
    codes_init,
    step_sizes,
    thresholds,
    active_ids,
    active_counts,
    owner_slots,
):
    tap_count = temporal_atoms.shape[1]
    rim_width = tap_count - 1
    atom_count, shard_len = codes_init.shape
    grp_size = lax.axis_size("grp")
    tm_index = lax.axis_index("tm")
    grp_index = lax.axis_index("grp")
    right_data = from_behind(recording[:, :rim_width], ("tm", "grp"), -1)
    extended = jnp.concatenate([recording, right_data], axis=1)
    projected = jnp.dot(spatial_maps, extended, preferred_element_type=jnp.float32)
    spatial_full = spatial_maps.astype(jnp.float32)
    gram_matrix = jnp.dot(spatial_full, spatial_full.T, precision=PRECISE)
    code_map = codes_init
    own_projected = projected[:, :shard_len]
    for sweep in range(ITERS):
        left_codes = from_behind(code_map[:, shard_len - rim_width :], ("tm", "grp"), 1)
        padded = jnp.concatenate([left_codes, code_map], axis=1)
        synthesis = depthwise(padded, temporal_atoms[:, ::-1])
        residual = own_projected - jnp.dot(gram_matrix, synthesis, precision=PRECISE)
        right_residual = from_behind(residual[:, :rim_width], ("tm", "grp"), -1)
        gradient = depthwise(jnp.concatenate([residual, right_residual], axis=1), temporal_atoms)
        code_map = jnp.maximum(code_map + step_sizes[:, None] * gradient - thresholds[:, None], 0.0)
    atom_ids = active_ids[0]
    live_count = active_counts[0]
    slot_count = atom_ids.shape[0]
    live_rows = (jnp.arange(slot_count) < live_count).astype(jnp.float32)
    selector = (atom_ids[:, None] == jnp.arange(atom_count)[None, :]).astype(
        jnp.float32
    ) * live_rows[:, None]
    picked = jnp.dot(selector, code_map, precision=PRECISE).astype(jnp.bfloat16)
    toeplitz = lagged(picked, tap_count)
    panel_rows = jnp.einsum("pt,alt->apl", extended, toeplitz, preferred_element_type=jnp.float32)
    panel_rows = (
        (panel_rows * float(shard_len) ** (-0.5)).astype(jnp.bfloat16).reshape(slot_count, -1)
    )
    block_size = atom_count // grp_size
    slot_tags = jnp.where(jnp.arange(slot_count) < live_count, atom_ids, -1).astype(jnp.bfloat16)
    all_panels, all_tags = (
        lax.all_gather(panel_rows, "grp", axis=0, tiled=True),
        lax.all_gather(slot_tags, "grp", axis=0, tiled=True),
    )
    wanted = (grp_index * block_size + jnp.arange(block_size)).astype(jnp.float32)
    chooser = (all_tags[None, :].astype(jnp.float32) == wanted[:, None]).astype(jnp.bfloat16)
    block_sums = jnp.dot(chooser, all_panels, preferred_element_type=jnp.float32)
    block_owner = lax.dynamic_slice_in_dim(owner_slots, grp_index * block_size, block_size)
    totals = lax.psum(block_sums, "tm")
    own_slots = tm_index * OWN + jnp.arange(OWN)
    picker = (block_owner[None, :] == own_slots[:, None]).astype(jnp.float32)
    owned_panels = jnp.dot(picker, totals, precision=PRECISE)
    return (code_map, owned_panels)


def solution(mesh):
    in_specs = (
        P(None, ("tm", "grp")),
        P(),
        P(),
        P(None, ("tm", "grp")),
        P(),
        P(),
        P(("tm", "grp"), None),
        P(("tm", "grp")),
        P(),
    )
    out_specs = (P(None, ("tm", "grp")), P(("tm", "grp"), None))
    return jax.shard_map(body, mesh=mesh, in_specs=in_specs, out_specs=out_specs, check_vma=False)
```

profile of v0, /device:TPU:1, one launch (start us, length us, event | category | flops | bytes accessed | tf_op | source)
XLA Modules:
  0.0 363.8 jit_solution(11805612218771303083)
XLA Ops:
  7.2 1.5 copy.27
  8.7 5.8 %collective-permute-start = (bf16[384,63]{0,1:T(8,128)(2,1)S(1)}, bf16[384,63]{0,1:T(8,128)(2,1)S(1)}, u32[]{:S(2)}, u32[]{:S(2)}) collective-permute-start(bf16[384,63]{0,1:T(8,128)(2,1)S(1)} %slice.300), channel_id=1, source_target_pairs={{1,0},{2,1},{3,2},{4,3},{5,4},{6,5},{7,6},{8,7},{9,8},{10,9},{11,1... | collective-permute-start | bytes 145160 | tf_op jit(solution)/shard_map/ppermute | solution.py:16
  15.4 1.9 collective-permute-start.1
  18.4 3.4 collective-permute-done.1
  23.7 2.6 convolution_select_fusion.5
  27.7 2.1 collective-permute-start.2
  29.9 2.5 collective-permute-done.2
  33.2 2.6 convolution_select_fusion.4
  36.6 2.1 collective-permute-start.3
  38.7 4.8 %collective-permute-done.3 = f32[64,63]{1,0:T(8,128)S(1)} collective-permute-done((f32[64,63]{1,0:T(8,128)S(1)}, f32[64,63]{1,0:T(8,128)S(1)}, u32[]{:S(2)}, u32[]{:S(2)}) %collective-permute-start.3) | collective-permute-done | bytes 16160 | tf_op jit(solution)/shard_map/ppermute | solution.py:16
  44.4 2.6 convolution_select_fusion.3
  48.0 4.5 %collective-permute-start.4 = (f32[64,63]{1,0:T(8,128)S(1)}, f32[64,63]{1,0:T(8,128)S(1)}, u32[]{:S(2)}, u32[]{:S(2)}) collective-permute-start(f32[64,63]{1,0:T(8,128)S(1)} %slice.310), channel_id=1, source_target_pairs={{1,0},{2,1},{3,2},{4,3},{5,4},{6,5},{7,6},{8,7},{9,8},{10,9},{11,1... | collective-permute-start | bytes 48392 | tf_op jit(solution)/shard_map/ppermute | solution.py:16
  54.3 2.6 convolution_select_fusion.2
  57.7 1.9 collective-permute-start.5
  60.2 4.5 %collective-permute-done.5 = f32[64,63]{1,0:T(8,128)S(1)} collective-permute-done((f32[64,63]{1,0:T(8,128)S(1)}, f32[64,63]{1,0:T(8,128)S(1)}, u32[]{:S(2)}, u32[]{:S(2)}) %collective-permute-start.5) | collective-permute-done | bytes 16160 | tf_op jit(solution)/shard_map/ppermute | solution.py:16
  65.6 2.6 convolution_select_fusion.1
  69.2 4.5 %collective-permute-start.6 = (f32[64,63]{1,0:T(8,128)S(1)}, f32[64,63]{1,0:T(8,128)S(1)}, u32[]{:S(2)}, u32[]{:S(2)}) collective-permute-start(f32[64,63]{1,0:T(8,128)S(1)} %slice.316), channel_id=1, source_target_pairs={{1,0},{2,1},{3,2},{4,3},{5,4},{6,5},{7,6},{8,7},{9,8},{10,9},{11,1... | collective-permute-start | bytes 48392 | tf_op jit(solution)/shard_map/ppermute | solution.py:16
  75.2 2.6 convolution_select_fusion
  86.9 2.1 reshape.27
  91.2 10.6 %all-reduce.1 = bf16[64]{0:T(256)(128)(2,1)S(1)} all-reduce(bf16[64]{0:T(256)(128)(2,1)S(1)} %dynamic-update-slice), channel_id=1, replica_groups=mesh['tm'=128,'grp'=4] {'grp'}, use_global_device_ids=true, to_apply=%add.1 | all-reduce | flops 64 | bytes 256
  101.9 49.2 %all-gather.2.cloned.1.call-done = bf16[64,24576]{1,0:T(8,128)(2,1)} async-done(((bf16[16,24576]{1,0:T(8,128)(2,1)}), bf16[64,24576]{1,0:T(8,128)(2,1)}) %all-gather.2.cloned.1.call-update) | async-done | bytes 3145744 | tf_op jit(solution)/shard_map/all_gather | solution.py:90
  151.0 3.6 %fusion.57 = f32[16,24576]{1,0:T(8,128)} fusion(bf16[64,24576]{1,0:T(8,128)(2,1)} %all-gather.2.cloned.1.call-done, f32[64]{0:T(128)S(1)} %convert_element_type.37, f32[16]{0:T(128)S(1)} %add_convert_fusion), kind=kOutput, calls=%fused_computation.144 | convolution fusion | flops 50332672 | bytes 4718912 | tf_op jit(solution)/shard_map/dot_general | solution.py:95
  154.8 199.5 %all-reduce.4.cloned.1.call-done = f32[16,24576]{1,0:T(8,128)} async-done(((f32[16,24576]{1,0:T(8,128)}), f32[16,24576]{1,0:T(8,128)}) %all-reduce.4.cloned.1.call-update) | async-done | bytes 1572880 | tf_op jit(solution)/shard_map/psum | solution.py:97
  354.2 2.7 fusion.64
  (165 shorter events, 25.2 us)
Async XLA Ops:
  7.2 10.1 %copy-start = (bf16[64,384]{1,0:T(8,128)(2,1)S(1)}, bf16[64,384]{1,0:T(8,128)(2,1)}, u32[]{:S(2)}) copy-start(bf16[64,384]{1,0:T(8,128)(2,1)} %param.10) | copy-start | bytes 147460
  7.2 143.8 %all-gather.2.cloned.1.call-start = ((), (), s32[]{:S(2)}) async-start(), calls=%async_computation | async-start | bytes 3932160 | tf_op jit(solution)/shard_map/all_gather | solution.py:90
  8.7 14.9 %copy-start.10 = (pred[8,136]{0,1:T(8,128)(4,1)S(1)}, pred[8,136]{0,1:T(8,128)(4,1)}, u32[]{:S(2)}) copy-start(pred[8,136]{0,1:T(8,128)(4,1)} %constant.66) | copy-start | bytes 3268
  8.7 18.1 %collective-permute-start = (bf16[384,63]{0,1:T(8,128)(2,1)S(1)}, bf16[384,63]{0,1:T(8,128)(2,1)S(1)}, u32[]{:S(2)}, u32[]{:S(2)}) collective-permute-start(bf16[384,63]{0,1:T(8,128)(2,1)S(1)} %slice.300), channel_id=1, source_target_pairs={{1,0},{2,1},{3,2},{4,3},{5,4},{6,5},{7,6},{8,7},{9,8},{10,9},{11,1... | collective-permute-start | bytes 145160 | tf_op jit(solution)/shard_map/ppermute | solution.py:16
  15.4 6.4 %collective-permute-start.1 = (f32[64,63]{1,0:T(8,128)S(1)}, f32[64,63]{1,0:T(8,128)S(1)}, u32[]{:S(2)}, u32[]{:S(2)}) collective-permute-start(f32[64,63]{1,0:T(8,128)S(1)} %slice.218), channel_id=1, source_target_pairs={{0,1},{1,2},{2,3},{3,4},{4,5},{5,6},{6,7},{7,8},{8,9},{9,10},{10,1... | collective-permute-start | bytes 48392 | tf_op jit(solution)/shard_map/ppermute | solution.py:16
  26.2 3.6 copy-start.3
  26.9 6.2 %copy-start.7 = (bf16[384,63]{0,1:T(8,128)(2,1)}, bf16[384,63]{0,1:T(8,128)(2,1)S(1)}, u32[]{:S(2)}) copy-start(bf16[384,63]{0,1:T(8,128)(2,1)S(1)} %collective-permute-done) | copy-start | bytes 145156
  27.7 4.7 %collective-permute-start.2 = (f32[64,63]{1,0:T(8,128)S(1)}, f32[64,63]{1,0:T(8,128)S(1)}, u32[]{:S(2)}, u32[]{:S(2)}) collective-permute-start(f32[64,63]{1,0:T(8,128)S(1)} %slice.304), channel_id=1, source_target_pairs={{1,0},{2,1},{3,2},{4,3},{5,4},{6,5},{7,6},{8,7},{9,8},{10,9},{11,1... | collective-permute-start | bytes 48392 | tf_op jit(solution)/shard_map/ppermute | solution.py:16
  33.1 3.2 copy-start.1
  33.1 3.2 copy-start.4
  33.1 3.2 copy-start.5
  36.6 6.9 %collective-permute-start.3 = (f32[64,63]{1,0:T(8,128)S(1)}, f32[64,63]{1,0:T(8,128)S(1)}, u32[]{:S(2)}, u32[]{:S(2)}) collective-permute-start(f32[64,63]{1,0:T(8,128)S(1)} %slice.307), channel_id=1, source_target_pairs={{0,1},{1,2},{2,3},{3,4},{4,5},{5,6},{6,7},{7,8},{8,9},{9,10},{10,1... | collective-permute-start | bytes 48392 | tf_op jit(solution)/shard_map/ppermute | solution.py:16
  48.0 5.5 %collective-permute-start.4 = (f32[64,63]{1,0:T(8,128)S(1)}, f32[64,63]{1,0:T(8,128)S(1)}, u32[]{:S(2)}, u32[]{:S(2)}) collective-permute-start(f32[64,63]{1,0:T(8,128)S(1)} %slice.310), channel_id=1, source_target_pairs={{1,0},{2,1},{3,2},{4,3},{5,4},{6,5},{7,6},{8,7},{9,8},{10,9},{11,1... | collective-permute-start | bytes 48392 | tf_op jit(solution)/shard_map/ppermute | solution.py:16
  57.7 7.0 %collective-permute-start.5 = (f32[64,63]{1,0:T(8,128)S(1)}, f32[64,63]{1,0:T(8,128)S(1)}, u32[]{:S(2)}, u32[]{:S(2)}) collective-permute-start(f32[64,63]{1,0:T(8,128)S(1)} %slice.313), channel_id=1, source_target_pairs={{0,1},{1,2},{2,3},{3,4},{4,5},{5,6},{6,7},{7,8},{8,9},{9,10},{10,1... | collective-permute-start | bytes 48392 | tf_op jit(solution)/shard_map/ppermute | solution.py:16
  69.2 5.2 %collective-permute-start.6 = (f32[64,63]{1,0:T(8,128)S(1)}, f32[64,63]{1,0:T(8,128)S(1)}, u32[]{:S(2)}, u32[]{:S(2)}) collective-permute-start(f32[64,63]{1,0:T(8,128)S(1)} %slice.316), channel_id=1, source_target_pairs={{1,0},{2,1},{3,2},{4,3},{5,4},{6,5},{7,6},{8,7},{9,8},{10,9},{11,1... | collective-permute-start | bytes 48392 | tf_op jit(solution)/shard_map/ppermute | solution.py:16
  77.8 0.8 copy-start.6
  78.5 6.0 %copy-start.2 = (f32[64,1024]{1,0:T(8,128)}, f32[64,1024]{1,0:T(8,128)S(1)}, u32[]{:S(2)}) copy-start(f32[64,1024]{1,0:T(8,128)S(1)} %fusion.47) | copy-start | bytes 786436
  78.5 6.0 %copy-start.8 = (bf16[384,63]{0,1:T(8,128)(2,1)S(1)}, bf16[384,63]{0,1:T(8,128)(2,1)}, u32[]{:S(2)}) copy-start(bf16[384,63]{0,1:T(8,128)(2,1)} %copy-done.7) | copy-start | bytes 145156
  89.0 265.3 %all-reduce.4.cloned.1.call-start = ((), (), s32[]{:S(2)}) async-start(), calls=%async_computation.1 | async-start | bytes 3145728 | tf_op jit(solution)/shard_map/psum | solution.py:97
  101.8 52.8 %copy-start.9 = (s32[64]{0:T(128)S(1)}, s32[64]{0:T(128)}, u32[]{:S(2)}) copy-start(s32[64]{0:T(128)} %param.17) | copy-start | bytes 772
Sparse Core Ops, SparseCore 0:
  89.1 61.8 all-gather.1
  154.8 199.3 all-reduce.3
where the time goes:
time: 365 us; the launch traced here: 364 us
  waiting for transfers between devices  266 us (73%)
  matrix products  25 us (7%)
  starting transfers between devices  22.9 us (6%)
  local copies, waits for them, and re-layouts  21.7 us (6%)
  between operations  16.2 us (4%)
  blocking collectives  10.6 us (3%)
    psum x1, waiting for transfers between devices, body(): totals = lax.psum(block_sums, 'tm')  199 us
    all_gather x1, waiting for transfers between devices, body(): lax.all_gather(panel_rows, 'grp', axis=0, tiled=True)  49.2 us
    ppermute x7, starting transfers between devices, from_behind(): return lax.ppermute(array, axis, pairs)  22.8 us
    ppermute x7, waiting for transfers between devices, from_behind(): return lax.ppermute(array, axis, pairs)  17 us
    conv_general_dilated x6, matrix products, depthwise(): lax.conv_general_dilated(signal[None], kernel[:, None, :], (1,), 'VALID',...  15.4 us
    unnamed x1, blocking collectives  10.6 us
    unnamed x89, local copies, waits for them, and re-layouts  8.49 us
    conv_general_dilated x30, local copies, waits for them, and re-layouts, depthwise(): lax.conv_general_dilated(signal[None], kernel[:, None, :], (1,), 'VALID',...  7.99 us
  transfers between devices with their start and end apart: 9, of which 8 were waited for; matrix products, arithmetic and copies ran while one was open for 2% of the time, Pallas kernels for 0%

commit v1 on v0

v1 whole, which is shorter than its diff:
```python
import functools

import jax
import jax.numpy as jnp
from jax import lax
from jax.experimental import pallas as pl
from jax.experimental.pallas import tpu as pltpu
from jax.sharding import PartitionSpec as P

ITERS = 3
OWN = 2
XN, YN, ZN, CN = 4, 8, 8, 2
HALO = 256
BF = jnp.bfloat16
F32 = jnp.float32
MESH = pl.DeviceIdType.MESH
VMEM = pl.BlockSpec(memory_space=pltpu.VMEM)


def dot(a, b, dims=((1,), (0,))):
    return lax.dot_general(a, b, (dims, ((), ())), preferred_element_type=F32)


def code_kernel(
    rec, maps, lags, codes0, step, thresh, select,
    codes_out, chunk,
    xb, pb, rech, send_sem, recv_sem,
):
    atoms, length = codes0.shape
    n_tm, n_grp = lax.axis_size("tm"), lax.axis_size("grp")
    shards = n_tm * n_grp
    shard = lax.axis_index("tm") * n_grp + lax.axis_index("grp")
    right, left = lax.rem(shard + 1, shards), lax.rem(shard + shards - 1, shards)
    right_id = (lax.div(right, n_grp), lax.rem(right, n_grp))
    left_id = (lax.div(left, n_grp), lax.rem(left, n_grp))

    barrier = pltpu.get_barrier_semaphore()
    for device in (left_id, right_id):
        pl.semaphore_signal(barrier, inc=1, device_id=device, device_id_type=MESH)
    pl.semaphore_wait(barrier, 2)

    def send(src, dst, index, device):
        copy = pltpu.make_async_remote_copy(
            src_ref=src,
            dst_ref=dst,
            send_sem=send_sem.at[index],
            recv_sem=recv_sem.at[index],
            device_id=device,
            device_id_type=MESH,
        )
        copy.start()
        return copy

    end = HALO + length
    width = end + HALO
    copies = [
        send(codes0.at[:, pl.ds(0, HALO)], xb.at[:, pl.ds(end, HALO)], 0, left_id),
        send(codes0.at[:, pl.ds(length - HALO, HALO)], xb.at[:, pl.ds(0, HALO)], 1, right_id),
    ]
    pb[:, HALO:end] = dot(maps[...], rec[...])
    copies += [
        send(pb.at[:, pl.ds(HALO, HALO)], pb.at[:, pl.ds(end, HALO)], 2, left_id),
        send(pb.at[:, pl.ds(end - 128, 128)], pb.at[:, pl.ds(128, 128)], 3, right_id),
        send(rec.at[:, pl.ds(0, 128)], rech, 4, left_id),
    ]
    xb[:, HALO:end] = codes0[...]

    gram = dot(maps[...], jnp.concatenate([maps[...]] * 8, axis=0), ((1,), (1,)))
    same = (
        lax.broadcasted_iota(jnp.int32, (atoms, 8 * atoms), 0)
        == lax.rem(lax.broadcasted_iota(jnp.int32, (atoms, 8 * atoms), 1), atoms)
    ).astype(F32)
    forward = jnp.concatenate([(gram * lags[i : i + 1, :]).astype(BF) for i in range(8)], axis=0)
    back = jnp.concatenate([(same * lags[i : i + 1, :]).astype(BF) for i in range(8)], axis=0)

    for copy in copies[:4]:
        copy.wait()

    first = jnp.where(shard == 0, HALO, 0)
    last = jnp.where(shard == shards - 1, end, width + HALO)

    def column(start, stop):
        return lax.broadcasted_iota(jnp.int32, (atoms, stop - start), 1) + start

    windows = [((128, width), (128, 1408)), ((128, 1408), (128, 1408)), ((HALO, 1408), (HALO, end))]
    x = jnp.where(column(0, width) < first, 0.0, xb[...])
    x_from = 0
    for (r_from, r_to), (c_from, c_to) in windows:
        x_bf = x.astype(BF)
        stacked = jnp.concatenate(
            [x_bf if j == 0 else pltpu.roll(x_bf, j, 1) for j in range(8)], axis=0
        )
        n = x.shape[1]
        z = dot(forward, stacked)
        y = z[:atoms]
        for i in range(1, 8):
            y = y + pltpu.roll(z[i * atoms : (i + 1) * atoms], 8 * i, 1)
        r = pb[:, r_from:r_to] - y[:, r_from - x_from : r_to - x_from]
        r = jnp.where(column(r_from, r_to) < last, r, 0.0)
        r_bf = r.astype(BF)
        n = r_to - r_from
        stacked = jnp.concatenate(
            [r_bf if j == 0 else pltpu.roll(r_bf, n - j, 1) for j in range(8)], axis=0
        )
        z = dot(back, stacked)
        g = z[:atoms]
        for i in range(1, 8):
            g = g + pltpu.roll(z[i * atoms : (i + 1) * atoms], n - 8 * i, 1)
        x = x[:, c_from - x_from : c_to - x_from]
        g = g[:, c_from - r_from : c_to - r_from]
        x = jnp.maximum(x + step[:, :1] * g - thresh[:, :1], 0.0)
        x = jnp.where(column(c_from, c_to) < first, 0.0, x)
        x_from = c_from
    codes_out[...] = x

    slots = select.shape[0]
    picked = dot(select[...], x.astype(BF)).astype(BF)
    picked = jnp.concatenate([picked, jnp.zeros((slots, 128), BF)], axis=1)
    shifted = jnp.concatenate(
        [picked if j == 0 else pltpu.roll(picked, j, 1) for j in range(16)], axis=0
    )
    copies[4].wait()
    after = jnp.where(shard == shards - 1, jnp.zeros_like(rech), rech[...])
    window = jnp.concatenate([rec[...], after], axis=1)
    n = length + 128
    for i in range(4):
        moved = window if i == 0 else pltpu.roll(window, n - 16 * i, 1)
        panel = dot(shifted, moved, ((1,), (1,)))
        panel = (panel * float(length) ** -0.5).astype(BF)
        for j in range(16):
            chunk[j % 8, 2 * i + j // 8] = panel[j * slots : (j + 1) * slots]


def run_codes(rec, maps, lags, codes0, step, thresh, select):
    atoms, length = codes0.shape
    channels = rec.shape[0]
    width = length + 2 * HALO
    slots = select.shape[0]
    return pl.pallas_call(
        code_kernel,
        out_shape=(
            jax.ShapeDtypeStruct((atoms, length), F32),
            jax.ShapeDtypeStruct((8, 8, slots, channels), BF),
        ),
        in_specs=[VMEM] * 7,
        out_specs=(VMEM, VMEM),
        scratch_shapes=[
            pltpu.VMEM((atoms, width), F32),
            pltpu.VMEM((atoms, width), F32),
            pltpu.VMEM((channels, 128), BF),
            pltpu.SemaphoreType.DMA((5,)),
            pltpu.SemaphoreType.DMA((5,)),
        ],
        compiler_params=pltpu.CompilerParams(
            collective_id=0, has_side_effects=True, vmem_limit_bytes=48 << 20
        ),
        name="codes",
    )(rec, maps, lags, codes0, step, thresh, select)


def sum_kernel(
    dims, chunk, tags, owners, out,
    recv1, tagr, send2, recv2, send3, recv3, tot, gath, recv5, send6, recv6,
    send_sem, recv_sem, local_sem,
):
    xn, yn, zn, cn = dims
    group = xn * cn
    atoms = send3.shape[0]
    slots = chunk.shape[2]
    block = atoms // xn
    part = atoms // zn
    tm = lax.axis_index("tm")
    x = lax.axis_index("grp")
    core = lax.rem(tm, cn)
    z = lax.rem(lax.div(tm, cn), zn)
    y = lax.div(tm, cn * zn)
    me = x * cn + core

    def device(yy, zz, cc, xx):
        return ((yy * zn + zz) * cn + cc, xx)

    pairs = []
    for o in range(1, group):
        xx, cc = lax.rem(x + o // cn, xn), lax.rem(core + o % cn, cn)
        pairs.append((xx * cn + cc, device(y, z, cc, xx)))
    ys = [lax.rem(y + o, yn) for o in range(1, yn)]
    zs = [lax.rem(z + o, zn) for o in range(1, zn)]

    barrier = pltpu.get_barrier_semaphore()
    partners = (
        [p for _, p in pairs]
        + [device(yy, z, core, x) for yy in ys]
        + [device(y, zz, core, x) for zz in zs]
    )
    for partner in partners:
        pl.semaphore_signal(barrier, inc=1, device_id=partner, device_id_type=MESH)
    pl.semaphore_wait(barrier, len(partners))

    started = []

    def send(src, dst, stage, index, target):
        copy = pltpu.make_async_remote_copy(
            src_ref=src,
            dst_ref=dst,
            send_sem=send_sem.at[stage, index],
            recv_sem=recv_sem.at[stage, index],
            device_id=target,
            device_id_type=MESH,
        )
        copy.start()
        started.append(copy)
        return copy

    first_tags = [send(tags, tagr.at[o], 0, o, p) for o, (_, p) in enumerate(pairs)]
    halves = []
    half = yn // 2
    for h in range(2):
        rows = pl.ds(h * half, half)
        own = pltpu.make_async_copy(chunk.at[me, rows], recv1.at[rows, me], local_sem.at[h])
        own.start()
        halves.append(
            [own]
            + [
                send(chunk.at[d, rows], recv1.at[rows, me], 1 + h, o, p)
                for o, (d, p) in enumerate(pairs)
            ]
        )
    for copy in first_tags:
        copy.wait_recv()
    lane = lax.broadcasted_iota(jnp.int32, (1, group * slots), 1)
    source = lax.div(lane, slots)
    row = jnp.where(source == me, tags[:1, : group * slots], -1.0)
    for o in range(1, group):
        frm = lax.rem(x - o // cn + xn, xn) * cn + lax.rem(core - o % cn + cn, cn)
        row = jnp.where(source == frm, tagr[o - 1, :1, : group * slots], row)
    atom = lax.broadcasted_iota(jnp.int32, (atoms, group * slots), 0).astype(F32)
    expand = (atom == row).astype(BF)

    for h in range(2):
        for copy in halves[h]:
            if copy is halves[h][0]:
                copy.wait()
            else:
                copy.wait_recv()
        for t in range(h * half, (h + 1) * half):
            terms = recv1[t].reshape(group * slots, recv1.shape[3])
            send2[t] = dot(expand, terms).astype(BF)
            @pl.when(y != t)
            def _():
                o = lax.rem(t - y + yn, yn) - 1
                pltpu.make_async_remote_copy(
                    src_ref=send2.at[t],
                    dst_ref=recv2.at[o],
                    send_sem=send_sem.at[3, o],
                    recv_sem=recv_sem.at[3, o],
                    device_id=device(t, z, core, x),
                    device_id_type=MESH,
                ).start()
    acc = send2[y].astype(F32)
    for o in range(yn - 1):
        copy = pltpu.make_async_remote_copy(
            src_ref=send2.at[0],
            dst_ref=recv2.at[o],
            send_sem=send_sem.at[3, o],
            recv_sem=recv_sem.at[3, o],
            device_id=device(ys[0], z, core, x),
            device_id_type=MESH,
        )
        copy.wait_recv()
        started.append(copy)
        acc = acc + recv2[o].astype(F32)
    send3[...] = acc

    third = [
        send(send3.at[pl.ds(zz * part, part)], recv3.at[o], 4, o, device(y, zz, core, x))
        for o, zz in enumerate(zs)
    ]
    mine = pl.ds(pl.multiple_of(z * part, part), part)
    acc = send3[mine]
    for o, copy in enumerate(third):
        copy.wait_recv()
        acc = acc + recv3[o]
    tot[...] = acc

    gath[mine] = acc
    fourth = [
        send(tot, gath.at[mine], 5, o, device(y, zz, core, x))
        for o, zz in enumerate(zs)
    ]
    for copy in fourth:
        copy.wait_recv()

    own = pltpu.make_async_copy(gath.at[pl.ds(x * block, block)], recv5.at[me], local_sem.at[2])
    own.start()
    fifth = [
        send(gath.at[pl.ds(lax.div(d, cn) * block, block)], recv5.at[me], 6, o, p)
        for o, (d, p) in enumerate(pairs)
    ]
    own.wait()
    for copy in fifth:
        copy.wait_recv()

    rows_n = yn * OWN * group
    cols_n = group * block
    r = lax.broadcasted_iota(jnp.int32, (rows_n, cols_n), 0)
    c = lax.broadcasted_iota(jnp.int32, (rows_n, cols_n), 1)
    wanted_y = lax.div(r, OWN * group)
    wanted_slot = lax.rem(lax.div(r, group), OWN)
    wanted = ((wanted_y * zn + z) * cn + core) * OWN + wanted_slot
    hit = (owners[:1, :cols_n] == wanted.astype(F32)) & (lax.rem(r, group) == lax.div(c, block))
    sums = recv5[...].reshape(cols_n, recv5.shape[2])
    rows = dot(hit.astype(BF), sums.astype(BF))
    send6[...] = rows.astype(BF).reshape(send6.shape)
    sixth = [
        send(send6.at[yy], recv6.at[y], 7, o, device(yy, z, core, x))
        for o, yy in enumerate(ys)
    ]
    recv6[y] = send6[y]
    for copy in sixth:
        copy.wait_recv()
    out[...] = recv6[...].astype(F32)
    for copy in started:
        copy.wait_send()


def run_sums(chunk, tags, owners, atoms, dims):
    xn, yn, zn, cn = dims
    group = xn * cn
    slots, channels = chunk.shape[2:]
    block = atoms // xn
    part = atoms // zn
    most = max(group, yn, zn) - 1
    return pl.pallas_call(
        functools.partial(sum_kernel, dims),
        out_shape=jax.ShapeDtypeStruct((yn, OWN * group, channels), F32),
        in_specs=[VMEM] * 3,
        out_specs=VMEM,
        scratch_shapes=[
            pltpu.VMEM((yn, group, slots, channels), BF),
            pltpu.VMEM((group - 1,) + tags.shape, F32),
            pltpu.VMEM((yn, atoms, channels), BF),
            pltpu.VMEM((yn - 1, atoms, channels), BF),
            pltpu.VMEM((atoms, channels), F32),
            pltpu.VMEM((zn - 1, part, channels), F32),
            pltpu.VMEM((part, channels), F32),
            pltpu.VMEM((atoms, channels), F32),
            pltpu.VMEM((group, block, channels), F32),
            pltpu.VMEM((yn, OWN * group, channels), BF),
            pltpu.VMEM((yn, OWN * group, channels), BF),
            pltpu.SemaphoreType.DMA((8, most)),
            pltpu.SemaphoreType.DMA((8, most)),
            pltpu.SemaphoreType.DMA((3,)),
        ],
        compiler_params=pltpu.CompilerParams(
            collective_id=1, has_side_effects=True, vmem_limit_bytes=48 << 20
        ),
        name="sums",
    )(chunk, tags, owners)


def body(
    recording,
    spatial_maps,
    temporal_atoms,
    codes_init,
    step_sizes,
    thresholds,
    active_ids,
    active_counts,
    owner_slots,
):
    atoms, taps = temporal_atoms.shape
    channels = recording.shape[0]
    dims = (XN, YN, ZN, CN)
    group = XN * CN
    block = atoms // XN
    slots = active_ids.shape[1]
    lags = temporal_atoms.T.reshape(8, 8 * atoms)
    live = jnp.arange(slots) < active_counts[0]
    ids = jnp.where(live, active_ids[0], -1)
    select = (ids[:, None] == jnp.arange(atoms)[None, :]).astype(BF)
    step = jnp.broadcast_to(step_sizes[:, None], (atoms, 128))
    thresh = jnp.broadcast_to(thresholds[:, None], (atoms, 128))
    tags = jnp.broadcast_to(jnp.tile(ids.astype(F32), group)[None, :], (8, group * slots))
    block_owner = lax.dynamic_slice_in_dim(owner_slots, lax.axis_index("grp") * block, block)
    owners = jnp.broadcast_to(
        jnp.tile(block_owner.astype(F32), group)[None, :], (8, group * block)
    )
    codes, chunk = run_codes(recording, spatial_maps, lags, codes_init, step, thresh, select)
    rows = run_sums(chunk, tags, owners, atoms, dims)
    panels = rows.reshape(YN, OWN, group, channels).transpose(1, 3, 0, 2)
    return codes, panels.reshape(OWN, channels * taps)


def solution(mesh):
    in_specs = (
        P(None, ("tm", "grp")),
        P(),
        P(),
        P(None, ("tm", "grp")),
        P(),
        P(),
        P(("tm", "grp"), None),
        P(("tm", "grp")),
        P(),
    )
    out_specs = (P(None, ("tm", "grp")), P(("tm", "grp"), None))
    return jax.shard_map(body, mesh=mesh, in_specs=in_specs, out_specs=out_specs, check_vma=False)
```

time: 365 us -> 92.2 us (0.25)
  waiting for transfers between devices: 266 us -> 0 us
  Pallas kernels: 0 us -> 75.9 us
  matrix products: 25 us -> 0 us
  starting transfers between devices: 22.9 us -> 0 us
  between operations: 16.2 us -> 1.31 us
  blocking collectives: 10.6 us -> 0 us
  local copies, waits for them, and re-layouts: 21.7 us -> 12.4 us
    psum x1 -> x0, waiting for transfers between devices: 199 us -> none  [body(): totals = lax.psum(block_sums, 'tm')]
    pallas_call x0 -> x2, Pallas kernels: none -> 75.9 us  [the longest x1 57.9 us: run_sums(): pl.pallas_call(functools.partial(sum_kernel, dims), out_shape=jax.ShapeDt...]
    all_gather x1 -> x0, waiting for transfers between devices: 49.2 us -> none  [body(): lax.all_gather(panel_rows, 'grp', axis=0, tiled=True)]
    ppermute x7 -> x0, starting transfers between devices: 22.8 us -> none  [from_behind(): return lax.ppermute(array, axis, pairs)]
    ppermute x7 -> x0, waiting for transfers between devices: 17 us -> none  [from_behind(): return lax.ppermute(array, axis, pairs)]
    conv_general_dilated x6 -> x0, matrix products: 15.4 us -> none  [depthwise(): lax.conv_general_dilated(signal[None], kernel[:, None, :], (1,), 'VALID',...]
    unnamed x1 -> x0, blocking collectives: 10.6 us -> none
    dot_general x9 -> x0, matrix products: 9.68 us -> none  [the longest x1 3.64 us: body(): jnp.dot(chooser, all_panels, preferred_element_type=jnp.float32)]
  transfers between devices with their start and end apart: 9 -> 0, of which waited for: 8 -> 0; matrix products, arithmetic and copies ran while one was open for 2% -> 0% of each run, Pallas kernels for 0% -> 0%
where the time goes in v1:
time: 92.2 us; the launch traced here: 91.8 us
  Pallas kernels  75.9 us (82%)
  local copies, waits for them, and re-layouts  12.4 us (13%)
  other arithmetic  2.13 us (2%)
  between operations  1.31 us (1%)
    pallas_call x1, Pallas kernels, run_sums(): pl.pallas_call(functools.partial(sum_kernel, dims), out_shape=jax.ShapeDt...  57.9 us
    pallas_call x1, Pallas kernels, run_codes(): pl.pallas_call(code_kernel, out_shape=(jax.ShapeDtypeStruct((atoms, lengt...  18 us
    reshape x1, local copies, waits for them, and re-layouts, body(): return (codes, panels.reshape(OWN, channels * taps))  4.13 us
    unnamed x7, local copies, waits for them, and re-layouts  3.59 us
    reshape x1, local copies, waits for them, and re-layouts, body(): panels = rows.reshape(YN, OWN, group, channels).transpose(1, 3, 0, 2)  2.17 us

profile of v1, /device:TPU:1, one launch (start us, length us, event | category | flops | bytes accessed | tf_op | source)
XLA Modules:
  0.0 91.8 jit_solution(7480024280509123481)
XLA Ops:
  1.3 0.7 dynamic-slice_convert_fusion
  2.0 0.7 fusion.2
  2.7 0.7 compare_select_fusion.1
  3.3 0.1 fusion.select
  3.4 0.1 broadcast_in_dim.38
  3.5 0.1 broadcast_in_dim.40
  3.6 0.8 copy.13
  4.4 0.1 reshape.34.lags
  4.5 0.7 broadcast_in_dim.34.step
  5.2 0.7 broadcast_in_dim.35.thresh
  6.0 0.0 copy-start
  6.0 1.1 %copy-done = bf16[384,1024]{1,0:T(8,128)(2,1)S(1)} copy-done((bf16[384,1024]{1,0:T(8,128)(2,1)S(1)}, bf16[384,1024]{1,0:T(8,128)(2,1)}, u32[]{:S(2)}) %copy-start) | copy-done | bytes 786456
  7.1 0.0 copy-start.1
  7.1 0.9 %copy-done.1 = f32[64,1024]{1,0:T(8,128)S(1)} copy-done((f32[64,1024]{1,0:T(8,128)S(1)}, f32[64,1024]{1,0:T(8,128)}, u32[]{:S(2)}) %copy-start.1) | copy-done | bytes 262168
  8.1 0.0 copy-start.2
  8.1 0.8 copy-done.2
  8.9 18.0 %codes.1 = (f32[64,1024]{1,0:T(8,128)S(1)}, bf16[8,8,16,384]{3,2,1,0:T(8,128)(2,1)S(1)}) custom-call(bf16[384,1024]{1,0:T(8,128)(2,1)S(1)} %copy-done, bf16[64,384]{1,0:T(8,128)(2,1)S(1)} %copy-done.2, f32[8,512]{1,0:T(8,128)S(1)} %reshape.34.lags, f32[64,1024]{1,0:T(8,128)S(1)} %copy-done.1, f32[64,128]{1,0:T(8,128)S(1)} %broadcast_in_dim.34.step, ...), custom_call_target="tpu_custom_call" | custom-call | tf_op jit(solution)/shard_map/codes/pallas_call | solution.py:139
  26.9 57.9 %sums.1 = f32[8,16,384]{2,1,0:T(8,128)S(1)} custom-call(bf16[8,8,16,384]{3,2,1,0:T(8,128)(2,1)S(1)} %get-tuple-element.5.chunk, f32[8,128]{1,0:T(8,128)S(1)} %broadcast_in_dim.39.tags, f32[8,128]{1,0:T(8,128)S(1)} %broadcast_in_dim.41.owners), custom_call_target="tpu_custom_call" | custom-call | tf_op jit(solution)/shard_map/sums/pallas_call | solution.py:333
  84.8 2.2 %copy.14 = f32[8,2,8,384]{2,0,3,1:T(8,128)} copy(f32[8,2,8,384]{3,2,1,0:T(8,128)S(1)} %bitcast.12) | data formatting | bytes 393216 | tf_op jit(solution)/shard_map/reshape | solution.py:391
  87.0 4.1 %reshape.36 = f32[2,24576]{1,0:T(2,128)} reshape(f32[2,384,8,8]{3,2,1,0:T(8,128)} %bitcast.13) | data formatting | bytes 393216 | tf_op jit(solution)/shard_map/reshape | solution.py:392
  91.1 0.7 copy.17
  (4 shorter events, 0.0 us)
Async XLA Ops:
  6.0 1.1 %copy-start = (bf16[384,1024]{1,0:T(8,128)(2,1)S(1)}, bf16[384,1024]{1,0:T(8,128)(2,1)}, u32[]{:S(2)}) copy-start(bf16[384,1024]{1,0:T(8,128)(2,1)} %rec.1) | copy-start | bytes 2359300
  7.1 0.9 %copy-start.1 = (f32[64,1024]{1,0:T(8,128)S(1)}, f32[64,1024]{1,0:T(8,128)}, u32[]{:S(2)}) copy-start(f32[64,1024]{1,0:T(8,128)} %codes0.1) | copy-start | bytes 786436
  8.1 0.8 copy-start.2

commit v2 on v0

v2 whole, which is shorter than its diff:
```python
import functools

import jax
import jax.numpy as jnp
from jax import lax
from jax.experimental import pallas as pl
from jax.experimental.pallas import tpu as pltpu
from jax.sharding import PartitionSpec as P

OWN = 2
XN, YN, ZN, CN = 4, 8, 8, 2
GROUP = XN * CN
HALO = 256
BF = jnp.bfloat16
F32 = jnp.float32
MESH = pl.DeviceIdType.MESH
HBM = pl.BlockSpec(memory_space=pl.ANY)
VMEM = pl.BlockSpec(memory_space=pltpu.VMEM)


def dot(a, b, dims=((1,), (0,))):
    return lax.dot_general(a, b, (dims, ((), ())), preferred_element_type=F32)


def split(v):
    high = v.astype(BF)
    return high, (v - high.astype(F32)).astype(BF)


def iota(shape, dim):
    return lax.broadcasted_iota(jnp.int32, shape, dim)


def to_column(row):
    n = row.shape[1]
    eye = iota((n, n), 0) == iota((n, n), 1)
    return jnp.sum(jnp.where(eye, jnp.broadcast_to(row, (n, n)), 0.0), axis=1, keepdims=True)


def kernel(
    rec_hbm, maps_hbm, waves_hbm, codes_hbm, step_hbm, thresh_hbm, ids_hbm, counts_hbm, owners_hbm,
    codes_out, panels_out,
    rec, maps, waves, step_row, thresh_row, ids_row, counts_row, owners_row,
    xb, pb, rech, tags, tagr, chunk, recv1, send2, recv2, send3, recv3, tot, recv4, send5, recv5,
    send6, recv6, turned, in_sem, send_sem, recv_sem,
):
    slots = ids_row.shape[1]
    channels, length = rec.shape
    atoms = maps.shape[0]
    block = atoms // XN
    part = atoms // ZN
    n_tm, n_grp = lax.axis_size("tm"), lax.axis_size("grp")
    shards = n_tm * n_grp
    tm = lax.axis_index("tm")
    x = lax.axis_index("grp")
    core = lax.rem(tm, CN)
    z = lax.rem(lax.div(tm, CN), ZN)
    y = lax.div(tm, CN * ZN)
    me = x * CN + core
    shard = tm * n_grp + x

    def device(yy, zz, cc, xx):
        return ((yy * ZN + zz) * CN + cc, xx)

    right, left = lax.rem(shard + 1, shards), lax.rem(shard + shards - 1, shards)
    right_id = (lax.div(right, n_grp), lax.rem(right, n_grp))
    left_id = (lax.div(left, n_grp), lax.rem(left, n_grp))
    pairs = []
    for o in range(1, GROUP):
        xx, cc = lax.rem(x + o // CN, XN), lax.rem(core + o % CN, CN)
        pairs.append((xx * CN + cc, device(y, z, cc, xx)))
    sibling = device(y, z, 1 - core, x)
    ys = [lax.rem(y + o, YN) for o in range(1, YN)]
    zs = [lax.rem(z + o, ZN) for o in range(1, ZN)]
    home = lax.div(z * part, block)
    per = block // part
    at_home = x == home

    barrier = pltpu.get_barrier_semaphore()

    def greet(target):
        pl.semaphore_signal(barrier, inc=1, device_id=target, device_id_type=MESH)

    partners = (
        [left_id, right_id]
        + [p for _, p in pairs]
        + [device(yy, z, core, x) for yy in ys]
        + [device(y, zz, core, x) for zz in zs]
    )
    for partner in partners:
        greet(partner)
    for xx in range(XN):
        for q in range(per):
            zz = x * per + q

            @pl.when(jnp.logical_not((x == xx) & (z == zz)))
            def _():
                greet(device(y, zz, core, xx))

    loads = [
        pltpu.make_async_copy(src, dst, in_sem.at[i])
        for i, (src, dst) in enumerate(
            [
                (codes_hbm, xb.at[:, pl.ds(HALO, length)]),
                (rec_hbm, rec),
                (maps_hbm, maps),
                (waves_hbm, waves),
                (step_hbm, step_row),
                (thresh_hbm, thresh_row),
                (ids_hbm, ids_row),
                (counts_hbm, counts_row),
                (owners_hbm, owners_row),
            ]
        )
    ]
    for load in loads:
        load.start()
    for load in loads:
        load.wait()

    started = []

    def copy_to(src, dst, stage, index, target, recv_index=None):
        return pltpu.make_async_remote_copy(
            src_ref=src,
            dst_ref=dst,
            send_sem=send_sem.at[stage, index],
            recv_sem=recv_sem.at[stage, index if recv_index is None else recv_index],
            device_id=target,
            device_id_type=MESH,
        )

    def send(*args):
        copy = copy_to(*args)
        copy.start()
        started.append(copy)
        return copy

    end = HALO + length
    width = end + HALO
    pb[:, HALO:end] = dot(maps[...], rec[...])
    pb[:, :128] = jnp.zeros((atoms, 128), F32)

    live = iota((1, slots), 1) < jnp.broadcast_to(counts_row[...], (1, slots))
    ids = jnp.where(live, ids_row[...].astype(F32), -1.0)
    tags[...] = jnp.broadcast_to(jnp.concatenate([ids] * GROUP, axis=1), tags.shape)
    select = (iota((slots, atoms), 1).astype(F32) == to_column(ids)).astype(BF)

    pl.semaphore_wait(barrier, len(partners) + ZN - jnp.where(at_home, 1, 0))

    halo = [
        send(xb.at[:, pl.ds(HALO, HALO)], xb.at[:, pl.ds(end, HALO)], 0, 0, left_id),
        send(xb.at[:, pl.ds(length, HALO)], xb.at[:, pl.ds(0, HALO)], 0, 1, right_id),
        send(pb.at[:, pl.ds(HALO, HALO)], pb.at[:, pl.ds(end, HALO)], 0, 2, left_id),
        send(pb.at[:, pl.ds(end - 128, 128)], pb.at[:, pl.ds(128, 128)], 0, 3, right_id),
    ]

    half = atoms // 2
    lanes = 8 * half
    pick_lag = iota((64, 8 * lanes), 1)
    pick_lag = lax.div(pick_lag, lanes) * 8 + lax.div(lax.rem(pick_lag, lanes), half)
    pick_lag = (pick_lag == iota((64, 8 * lanes), 0)).astype(BF)
    same = (iota((half, lanes), 0) == lax.rem(iota((half, lanes), 1), half)).astype(F32)
    spread = [dot(v, pick_lag) for v in split(waves[...])]
    filters = []
    for g in range(2):
        high, low = [
            jnp.concatenate(
                [
                    (v[g * half : (g + 1) * half, i * lanes : (i + 1) * lanes] * same).astype(BF)
                    for i in range(8)
                ],
                axis=0,
            )
            for v in spread
        ]
        filters.append(jnp.concatenate([high, high, low], axis=1))
    high, low = split(dot(maps[...], maps[...], ((1,), (1,))))
    gram = jnp.concatenate([high, high, low], axis=1)
    step = to_column(step_row[...])
    thresh = to_column(thresh_row[...])

    def depthwise(v, sign):
        n = v.shape[1]
        rolled = [
            [u if j == 0 else pltpu.roll(u, (sign * j) % n, 1) for j in range(8)] for u in split(v)
        ]
        groups = []
        for g in range(2):
            high, low = [
                jnp.concatenate([u[g * half : (g + 1) * half] for u in us], axis=0) for us in rolled
            ]
            w = dot(filters[g], jnp.concatenate([high, low, high], axis=0))
            total = w[:half]
            for i in range(1, 8):
                total = total + pltpu.roll(w[i * half : (i + 1) * half], (sign * 8 * i) % n, 1)
            groups.append(total)
        return jnp.concatenate(groups, axis=0)

    for copy in halo:
        copy.wait_recv()
    more = [
        send(rec.at[:, pl.ds(0, 128)], rech, 0, 4, left_id),
    ]
    tag_copies = [send(tags, tagr.at[o], 1, o, p) for o, (_, p) in enumerate(pairs)]

    first = jnp.where(shard == 0, HALO, 0)
    last = jnp.where(shard == shards - 1, end, width + HALO)

    def column(start, stop):
        return iota((atoms, stop - start), 1) + start

    windows = [((128, width), (128, 1408)), ((128, 1408), (128, 1408)), ((HALO, 1408), (HALO, end))]
    v = jnp.where(column(0, width) < first, 0.0, xb[...])
    v_from = 0
    for (r_from, r_to), (c_from, c_to) in windows:
        synthesis = depthwise(v, 1)[:, r_from - v_from : r_to - v_from]
        high, low = split(synthesis)
        r = pb[:, r_from:r_to] - dot(gram, jnp.concatenate([high, low, high], axis=0))
        r = jnp.where(column(r_from, r_to) < last, r, 0.0)
        g = depthwise(r, -1)[:, c_from - r_from : c_to - r_from]
        v = v[:, c_from - v_from : c_to - v_from]
        v = jnp.maximum(v + step * g - thresh, 0.0)
        v = jnp.where(column(c_from, c_to) < first, 0.0, v)
        v_from = c_from
    codes_out[...] = v

    picked = dot(select, v.astype(BF)).astype(BF)
    picked = jnp.concatenate([picked, jnp.zeros((slots, 128), BF)], axis=1)
    shifted = jnp.concatenate(
        [picked if j == 0 else pltpu.roll(picked, j, 1) for j in range(16)], axis=0
    )
    more[0].wait_recv()
    after = jnp.where(shard == shards - 1, jnp.zeros_like(rech), rech[...])
    window = jnp.concatenate([rec[...], after], axis=1)
    n = length + 128
    pieces = YN // 2
    order = [lax.rem(lax.div(y, 2) + p + 1, pieces) for p in range(pieces)]
    firsts = []
    for p in range(pieces):
        i = order[p]
        moved = pltpu.roll(window, lax.rem(n - 16 * i, n), 1)
        panel = dot(shifted, moved, ((1,), (1,)))
        panel = (panel * float(length) ** -0.5).astype(BF)
        for j in range(16):
            chunk[j % 8, 2 * i + j // 8] = panel[j * slots : (j + 1) * slots]
        rows = pl.ds(2 * i, 2)
        firsts.append(
            [
                send(chunk.at[d, rows], recv1.at[rows, me], 2 + p, o, target)
                for o, (d, target) in enumerate(pairs)
            ]
        )
        recv1[rows, me] = chunk[me, rows]

    for copy in tag_copies:
        copy.wait_recv()
    lane = iota((1, GROUP * slots), 1)
    source = lax.div(lane, slots)
    row = jnp.where(source == me, tags[:1], -1.0)
    for o in range(1, GROUP):
        frm = lax.rem(x - o // CN + XN, XN) * CN + lax.rem(core - o % CN + CN, CN)
        row = jnp.where(source == frm, tagr[o - 1, :1], row)
    expand = (iota((atoms, GROUP * slots), 0).astype(F32) == row).astype(BF)
    for p in range(pieces):
        for copy in firsts[p]:
            copy.wait_recv()
        for q in range(2):
            t = 2 * order[p] + q
            terms = recv1[t].reshape(GROUP * slots, channels)
            send2[t] = dot(expand, terms).astype(BF)
            o = lax.rem(t - y + YN, YN)

            @pl.when(o != 0)
            def _():
                copy_to(send2.at[t], recv2.at[o - 1], 6, o - 1, device(t, z, core, x)).start()

    acc = send2[y].astype(F32)
    for o in range(YN - 1):
        copy = copy_to(send2.at[0], recv2.at[o], 6, o, device(ys[0], z, core, x))
        copy.wait_recv()
        started.append(copy)
        acc = acc + recv2[o].astype(F32)
    send3[...] = acc

    third = [
        send(send3.at[pl.ds(zz * part, part)], recv3.at[o], 7, o, device(y, zz, core, x))
        for o, zz in enumerate(zs)
    ]
    acc = send3[pl.ds(pl.multiple_of(z * part, part), part)]
    for o, copy in enumerate(third):
        copy.wait_recv()
        acc = acc + recv3[o]
    tot[...] = acc

    place = x * per + lax.rem(z, per)
    fourth = []
    for o in range(ZN):
        zz = lax.rem(z + o, ZN)
        copy = copy_to(tot, recv4.at[place], 8, o, device(y, zz, core, home), place)
        fourth.append(copy)
        if o == 0:

            @pl.when(jnp.logical_not(at_home))
            def _():
                copy.start()

            @pl.when(at_home)
            def _():
                recv4[place] = tot[...]
        else:
            copy.start()
    for xx in range(XN):
        for q in range(per):
            k = xx * per + q
            copy = copy_to(tot, recv4.at[k], 8, 0, sibling, k)

            @pl.when(jnp.logical_not((x == xx) & (z == x * per + q)))
            def _():
                copy.wait_recv()

    send5[...] = recv4[...].reshape(XN * block, channels).astype(BF)
    fifth = send(send5, recv5, 9, 0, sibling)
    rows_n = YN * OWN * GROUP
    cols_n = GROUP * block
    half_n = XN * block
    block_owner = owners_row[:, :block]
    for b in range(1, XN):
        block_owner = jnp.where(x == b, owners_row[:, b * block : (b + 1) * block], block_owner)
    block_owner = jnp.concatenate([block_owner.astype(F32)] * GROUP, axis=1)
    r = iota((rows_n, cols_n), 0)
    c = iota((rows_n, cols_n), 1)
    wanted_slot = lax.rem(lax.div(r, GROUP), OWN)
    wanted = ((lax.div(r, OWN * GROUP) * ZN + z) * CN + core) * OWN + wanted_slot
    c_core = jnp.where(c < half_n, core, 1 - core)
    c_group = lax.div(lax.rem(c, half_n), block) * CN + c_core
    hit = (block_owner == wanted.astype(F32)) & (lax.rem(r, GROUP) == c_group)
    hit = hit.astype(BF)
    fifth.wait_recv()

    sums = jnp.concatenate([send5[...], recv5[...]], axis=0)
    send6[...] = dot(hit, sums).astype(BF).reshape(send6.shape)
    sixth = [
        send(send6.at[yy], recv6.at[y], 10, o, device(yy, z, core, x)) for o, yy in enumerate(ys)
    ]
    recv6[y] = send6[y]
    for copy in sixth:
        copy.wait_recv()

    held = recv6[...].astype(F32)
    taps = YN * GROUP
    table = jnp.concatenate(
        [held[:, s * GROUP : (s + 1) * GROUP].reshape(taps, channels) for s in range(OWN)], axis=0
    )
    turned[...] = table.T
    even = turned[pl.ds(0, channels // 2, stride=2), :]
    odd = turned[pl.ds(1, channels // 2, stride=2), :]
    low_lanes = iota(even.shape, 1) < taps
    slot0 = jnp.where(low_lanes, even, pltpu.roll(odd, taps, 1))
    slot1 = jnp.where(low_lanes, pltpu.roll(even, taps, 1), odd)
    for q in range(channels // 2):
        panels_out[:, q * 128 : (q + 1) * 128] = jnp.concatenate(
            [slot0[q : q + 1], slot1[q : q + 1]], axis=0
        )

    for copy in started:
        copy.wait_send()
    for o, copy in enumerate(fourth):
        if o == 0:

            @pl.when(jnp.logical_not(at_home))
            def _():
                copy.wait_send()
        else:
            copy.wait_send()


def body(
    recording,
    spatial_maps,
    temporal_atoms,
    codes_init,
    step_sizes,
    thresholds,
    active_ids,
    active_counts,
    owner_slots,
):
    atoms, taps = temporal_atoms.shape
    channels, length = recording.shape
    slots = active_ids.shape[1]
    width = length + 2 * HALO
    block, part = atoms // XN, atoms // ZN
    return pl.pallas_call(
        kernel,
        out_shape=(
            jax.ShapeDtypeStruct((atoms, length), F32),
            jax.ShapeDtypeStruct((OWN, channels * taps), F32),
        ),
        in_specs=[HBM] * 9,
        out_specs=(VMEM, VMEM),
        scratch_shapes=[
            pltpu.VMEM((channels, length), BF),
            pltpu.VMEM((atoms, channels), BF),
            pltpu.VMEM((atoms, taps), F32),
            pltpu.VMEM((1, atoms), F32),
            pltpu.VMEM((1, atoms), F32),
            pltpu.VMEM((1, slots), jnp.int32),
            pltpu.VMEM((1, 1), jnp.int32),
            pltpu.VMEM((1, atoms), jnp.int32),
            pltpu.VMEM((atoms, width), F32),
            pltpu.VMEM((atoms, width), F32),
            pltpu.VMEM((channels, 128), BF),
            pltpu.VMEM((8, GROUP * slots), F32),
            pltpu.VMEM((GROUP - 1, 8, GROUP * slots), F32),
            pltpu.VMEM((GROUP, YN, slots, channels), BF),
            pltpu.VMEM((YN, GROUP, slots, channels), BF),
            pltpu.VMEM((YN, atoms, channels), BF),
            pltpu.VMEM((YN - 1, atoms, channels), BF),
            pltpu.VMEM((atoms, channels), F32),
            pltpu.VMEM((ZN - 1, part, channels), F32),
            pltpu.VMEM((part, channels), F32),
            pltpu.VMEM((XN * block // part, part, channels), F32),
            pltpu.VMEM((XN * block, channels), BF),
            pltpu.VMEM((XN * block, channels), BF),
            pltpu.VMEM((YN, OWN * GROUP, channels), BF),
            pltpu.VMEM((YN, OWN * GROUP, channels), BF),
            pltpu.VMEM((channels, OWN * taps), F32),
            pltpu.SemaphoreType.DMA((9,)),
            pltpu.SemaphoreType.DMA((11, 8)),
            pltpu.SemaphoreType.DMA((11, 8)),
        ],
        compiler_params=pltpu.CompilerParams(
            collective_id=0, has_side_effects=True, vmem_limit_bytes=56 << 20
        ),
        name="codes_and_panels",
    )(
        recording,
        spatial_maps,
        temporal_atoms,
        codes_init,
        step_sizes.reshape(1, atoms),
        thresholds.reshape(1, atoms),
        active_ids,
        active_counts.reshape(1, 1),
        owner_slots.reshape(1, atoms),
    )


def solution(mesh):
    in_specs = (
        P(None, ("tm", "grp")),
        P(),
        P(),
        P(None, ("tm", "grp")),
        P(),
        P(),
        P(("tm", "grp"), None),
        P(("tm", "grp")),
        P(),
    )
    out_specs = (P(None, ("tm", "grp")), P(("tm", "grp"), None))
    return jax.shard_map(body, mesh=mesh, in_specs=in_specs, out_specs=out_specs, check_vma=False)
```

time: 365 us -> 72.1 us (0.20)
  waiting for transfers between devices: 266 us -> 0 us
  Pallas kernels: 0 us -> 68.2 us
  matrix products: 25 us -> 0 us
  starting transfers between devices: 22.9 us -> 0 us
  local copies, waits for them, and re-layouts: 21.7 us -> 2.39 us
  between operations: 16.2 us -> 1.3 us
  blocking collectives: 10.6 us -> 0 us
    psum x1 -> x0, waiting for transfers between devices: 199 us -> none  [body(): totals = lax.psum(block_sums, 'tm')]
    pallas_call x0 -> x1, Pallas kernels: none -> 68.2 us  [body(): pl.pallas_call(kernel, out_shape=(jax.ShapeDtypeStruct((atoms, length), F...]
    all_gather x1 -> x0, waiting for transfers between devices: 49.2 us -> none  [body(): lax.all_gather(panel_rows, 'grp', axis=0, tiled=True)]
    ppermute x7 -> x0, starting transfers between devices: 22.8 us -> none  [from_behind(): return lax.ppermute(array, axis, pairs)]
    ppermute x7 -> x0, waiting for transfers between devices: 17 us -> none  [from_behind(): return lax.ppermute(array, axis, pairs)]
    conv_general_dilated x6 -> x0, matrix products: 15.4 us -> none  [depthwise(): lax.conv_general_dilated(signal[None], kernel[:, None, :], (1,), 'VALID',...]
    unnamed x1 -> x0, blocking collectives: 10.6 us -> none
    dot_general x9 -> x0, matrix products: 9.68 us -> none  [the longest x1 3.64 us: body(): jnp.dot(chooser, all_panels, preferred_element_type=jnp.float32)]
  transfers between devices with their start and end apart: 9 -> 0, of which waited for: 8 -> 0; matrix products, arithmetic and copies ran while one was open for 2% -> 0% of each run, Pallas kernels for 0% -> 0%
where the time goes in v2:
time: 72.1 us; the launch traced here: 71.9 us
  Pallas kernels  68.2 us (95%)
  local copies, waits for them, and re-layouts  2.39 us (3%)
  between operations  1.3 us (2%)
    pallas_call x1, Pallas kernels, body(): pl.pallas_call(kernel, out_shape=(jax.ShapeDtypeStruct((atoms, length), F...  68.2 us
    unnamed x4, local copies, waits for them, and re-layouts  2.39 us

profile of v2, /device:TPU:1, one launch (start us, length us, event | category | flops | bytes accessed | tf_op | source)
XLA Modules:
  0.0 71.9 jit_solution(2168329954957697819)
XLA Ops:
  1.3 68.2 %codes_and_panels.1 = (f32[64,1024]{1,0:T(8,128)}, f32[2,24576]{1,0:T(2,128)}) custom-call(bf16[384,1024]{1,0:T(8,128)(2,1)} %rec_hbm.1, bf16[64,384]{1,0:T(8,128)(2,1)} %maps_hbm.1, f32[64,64]{1,0:T(8,128)} %waves_hbm.1, f32[64,1024]{1,0:T(8,128)} %codes_hbm.1, f32[1,64]{1,0:T(1,128)} %bitcast.5, f32[1,64]{1,0:T(1,128)} %bitcast.6, s32[1,16]{1,0:T(1,128)} %ids_hbm.1, ...), custom_call_target="tpu_custom_call" | custom-call | tf_op jit(solution)/shard_map/codes_and_panels/pallas_call | solution.py:394
  69.5 0.0 copy-start
  69.5 1.7 %copy.14 = f32[64,1024]{1,0:T(8,128)} copy(f32[64,1024]{1,0:T(8,128)} %get-tuple-element.4) | data formatting | bytes 524288
  71.2 0.0 copy-done
  71.2 0.7 copy.15
Async XLA Ops:
  69.5 1.7 %copy-start = (f32[2,24576]{1,0:T(2,128)S(1)}, f32[2,24576]{1,0:T(2,128)}, u32[]{:S(2)}) copy-start(f32[2,24576]{1,0:T(2,128)} %get-tuple-element.5) | copy-start | bytes 589828

commit v3 on v2

--- a/solution.py
+++ b/solution.py
@@ -115,8 +115,6 @@
     ]
     for load in loads:
         load.start()
-    for load in loads:
-        load.wait()
 
     started = []
 
@@ -138,22 +136,24 @@
 
     end = HALO + length
     width = end + HALO
+    pl.semaphore_wait(barrier, len(partners) + ZN - jnp.where(at_home, 1, 0))
+    halo = [
+        send(codes_hbm.at[:, pl.ds(0, HALO)], xb.at[:, pl.ds(end, HALO)], 0, 0, left_id),
+        send(codes_hbm.at[:, pl.ds(length - HALO, HALO)], xb.at[:, pl.ds(0, HALO)], 0, 1, right_id),
+    ]
+    for load in loads:
+        load.wait()
     pb[:, HALO:end] = dot(maps[...], rec[...])
+    halo += [
+        send(pb.at[:, pl.ds(HALO, HALO)], pb.at[:, pl.ds(end, HALO)], 0, 2, left_id),
+        send(pb.at[:, pl.ds(end - 128, 128)], pb.at[:, pl.ds(128, 128)], 0, 3, right_id),
+    ]
     pb[:, :128] = jnp.zeros((atoms, 128), F32)
 
     live = iota((1, slots), 1) < jnp.broadcast_to(counts_row[...], (1, slots))
     ids = jnp.where(live, ids_row[...].astype(F32), -1.0)
     tags[...] = jnp.broadcast_to(jnp.concatenate([ids] * GROUP, axis=1), tags.shape)
     select = (iota((slots, atoms), 1).astype(F32) == to_column(ids)).astype(BF)
-
-    pl.semaphore_wait(barrier, len(partners) + ZN - jnp.where(at_home, 1, 0))
-
-    halo = [
-        send(xb.at[:, pl.ds(HALO, HALO)], xb.at[:, pl.ds(end, HALO)], 0, 0, left_id),
-        send(xb.at[:, pl.ds(length, HALO)], xb.at[:, pl.ds(0, HALO)], 0, 1, right_id),
-        send(pb.at[:, pl.ds(HALO, HALO)], pb.at[:, pl.ds(end, HALO)], 0, 2, left_id),
-        send(pb.at[:, pl.ds(end - 128, 128)], pb.at[:, pl.ds(128, 128)], 0, 3, right_id),
-    ]
 
     half = atoms // 2
     lanes = 8 * half
@@ -375,6 +375,11 @@
             copy.wait_send()
 
 
+def finish(codes_in, panels_in, codes_out, panels_out):
+    codes_out[...] = codes_in[...]
+    panels_out[...] = panels_in[...]
+
+
 def body(
     recording,
     spatial_maps,
@@ -391,12 +396,13 @@
     slots = active_ids.shape[1]
     width = length + 2 * HALO
     block, part = atoms // XN, atoms // ZN
-    return pl.pallas_call(
+    shapes = (
+        jax.ShapeDtypeStruct((atoms, length), F32),
+        jax.ShapeDtypeStruct((OWN, channels * taps), F32),
+    )
+    results = pl.pallas_call(
         kernel,
-        out_shape=(
-            jax.ShapeDtypeStruct((atoms, length), F32),
-            jax.ShapeDtypeStruct((OWN, channels * taps), F32),
-        ),
+        out_shape=shapes,
         in_specs=[HBM] * 9,
         out_specs=(VMEM, VMEM),
         scratch_shapes=[
@@ -445,6 +451,13 @@
         active_counts.reshape(1, 1),
         owner_slots.reshape(1, atoms),
     )
+    return pl.pallas_call(
+        finish,
+        out_shape=shapes,
+        in_specs=[VMEM] * 2,
+        out_specs=(VMEM, VMEM),
+        name="finish",
+    )(*results)
 
 
 def solution(mesh):

time: 72.1 us -> 71.6 us (level)
  local copies, waits for them, and re-layouts: 2.39 us -> 0 us
  Pallas kernels: 68.2 us -> 70.2 us
    unnamed x4 -> x0, local copies, waits for them, and re-layouts: 2.39 us -> none
    pallas_call x1 -> x2, Pallas kernels: 68.2 us -> 70.2 us  [the longest x1 68.4 us: body(): pl.pallas_call(kernel, out_shape=shapes, in_specs=[HBM] * 9, out_specs=(V...]
where the time goes in v3:
time: 71.6 us; the launch traced here: 71.5 us
  Pallas kernels  70.2 us (98%)
  between operations  1.29 us (2%)
    pallas_call x1, Pallas kernels, body(): pl.pallas_call(kernel, out_shape=shapes, in_specs=[HBM] * 9, out_specs=(V...  68.4 us
    pallas_call x1, Pallas kernels, body(): pl.pallas_call(finish, out_shape=shapes, in_specs=[VMEM] * 2, out_specs=(...  1.79 us

profile of v3, /device:TPU:1, one launch (start us, length us, event | category | flops | bytes accessed | tf_op | source)
XLA Modules:
  0.0 71.5 jit_solution(15658902937687805815)
XLA Ops:
  1.3 68.4 %codes_and_panels.1 = (f32[64,1024]{1,0:T(8,128)}, f32[2,24576]{1,0:T(2,128)}) custom-call(bf16[384,1024]{1,0:T(8,128)(2,1)} %rec_hbm.1, bf16[64,384]{1,0:T(8,128)(2,1)} %maps_hbm.1, f32[64,64]{1,0:T(8,128)} %waves_hbm.1, f32[64,1024]{1,0:T(8,128)} %codes_hbm.1, f32[1,64]{1,0:T(1,128)} %bitcast.5, f32[1,64]{1,0:T(1,128)} %bitcast.6, s32[1,16]{1,0:T(1,128)} %ids_hbm.1, ...), custom_call_target="tpu_custom_call" | custom-call | tf_op jit(solution)/shard_map/codes_and_panels/pallas_call | solution.py:403
  69.7 1.8 %finish.1 = (f32[64,1024]{1,0:T(8,128)}, f32[2,24576]{1,0:T(2,128)}) custom-call(f32[64,1024]{1,0:T(8,128)} %get-tuple-element.4.codes_in, f32[2,24576]{1,0:T(2,128)} %get-tuple-element.5.panels_in), custom_call_target="tpu_custom_call" | custom-call | tf_op jit(solution)/shard_map/finish/pallas_call | solution.py:454

commit v4 on v3

--- a/solution.py
+++ b/solution.py
@@ -41,8 +41,8 @@
     rec_hbm, maps_hbm, waves_hbm, codes_hbm, step_hbm, thresh_hbm, ids_hbm, counts_hbm, owners_hbm,
     codes_out, panels_out,
     rec, maps, waves, step_row, thresh_row, ids_row, counts_row, owners_row,
-    xb, pb, rech, tags, tagr, chunk, recv1, send2, recv2, send3, recv3, tot, recv4, send5, recv5,
-    send6, recv6, turned, in_sem, send_sem, recv_sem,
+    xb, pb, rech, tags, tagr, chunk, recv1, send2, recv2, tot, recv4, send5, recv5,
+    send6, recv6, turned, in_sem, send_sem, recv_sem, plane_send, plane_recv,
 ):
     slots = ids_row.shape[1]
     channels, length = rec.shape
@@ -71,7 +71,9 @@
         pairs.append((xx * CN + cc, device(y, z, cc, xx)))
     sibling = device(y, z, 1 - core, x)
     ys = [lax.rem(y + o, YN) for o in range(1, YN)]
-    zs = [lax.rem(z + o, ZN) for o in range(1, ZN)]
+    plane = []
+    for o in range(1, YN * ZN):
+        plane.append(device(lax.rem(y + o // ZN, YN), lax.rem(z + o % ZN, ZN), core, x))
     home = lax.div(z * part, block)
     per = block // part
     at_home = x == home
@@ -84,8 +86,7 @@
     partners = (
         [left_id, right_id]
         + [p for _, p in pairs]
-        + [device(yy, z, core, x) for yy in ys]
-        + [device(y, zz, core, x) for zz in zs]
+        + plane
     )
     for partner in partners:
         greet(partner)
@@ -197,13 +198,8 @@
             groups.append(total)
         return jnp.concatenate(groups, axis=0)
 
-    for copy in halo:
+    for copy in halo[:2]:
         copy.wait_recv()
-    more = [
-        send(rec.at[:, pl.ds(0, 128)], rech, 0, 4, left_id),
-    ]
-    tag_copies = [send(tags, tagr.at[o], 1, o, p) for o, (_, p) in enumerate(pairs)]
-
     first = jnp.where(shard == 0, HALO, 0)
     last = jnp.where(shard == shards - 1, end, width + HALO)
 
@@ -216,7 +212,13 @@
     for (r_from, r_to), (c_from, c_to) in windows:
         synthesis = depthwise(v, 1)[:, r_from - v_from : r_to - v_from]
         high, low = split(synthesis)
-        r = pb[:, r_from:r_to] - dot(gram, jnp.concatenate([high, low, high], axis=0))
+        mixed = dot(gram, jnp.concatenate([high, low, high], axis=0))
+        if v_from == 0:
+            for copy in halo[2:]:
+                copy.wait_recv()
+            more = [send(rec.at[:, pl.ds(0, 128)], rech, 0, 4, left_id)]
+            tag_copies = [send(tags, tagr.at[o], 1, o, p) for o, (_, p) in enumerate(pairs)]
+        r = pb[:, r_from:r_to] - mixed
         r = jnp.where(column(r_from, r_to) < last, r, 0.0)
         g = depthwise(r, -1)[:, c_from - r_from : c_to - r_from]
         v = v[:, c_from - v_from : c_to - v_from]
@@ -253,6 +255,23 @@
         )
         recv1[rows, me] = chunk[me, rows]
 
+    wide = recv2.shape[2]
+
+    def part_of(t, zz):
+        rows = pl.multiple_of(lax.div(zz, per) * block, block)
+        cols = pl.multiple_of(lax.rem(zz, per) * (channels - wide), 128)
+        return send2.at[t, pl.ds(rows, block), pl.ds(cols, wide)]
+
+    def plane_copy(src, o, target):
+        return pltpu.make_async_remote_copy(
+            src_ref=src,
+            dst_ref=recv2.at[o - 1],
+            send_sem=plane_send.at[o - 1],
+            recv_sem=plane_recv.at[o - 1],
+            device_id=target,
+            device_id_type=MESH,
+        )
+
     for copy in tag_copies:
         copy.wait_recv()
     lane = iota((1, GROUP * slots), 1)
@@ -269,29 +288,21 @@
             t = 2 * order[p] + q
             terms = recv1[t].reshape(GROUP * slots, channels)
             send2[t] = dot(expand, terms).astype(BF)
-            o = lax.rem(t - y + YN, YN)
-
-            @pl.when(o != 0)
-            def _():
-                copy_to(send2.at[t], recv2.at[o - 1], 6, o - 1, device(t, z, core, x)).start()
-
-    acc = send2[y].astype(F32)
-    for o in range(YN - 1):
-        copy = copy_to(send2.at[0], recv2.at[o], 6, o, device(ys[0], z, core, x))
+            for k in range(ZN):
+                zz = lax.rem(z + k, ZN)
+                o = lax.rem(t - y + YN, YN) * ZN + k
+
+                @pl.when(o != 0)
+                def _():
+                    plane_copy(part_of(t, zz), o, device(t, zz, core, x)).start()
+
+    acc = part_of(y, z)[...].astype(F32)
+    for o in range(1, YN * ZN):
+        copy = plane_copy(part_of(0, 0), o, plane[o - 1])
         copy.wait_recv()
         started.append(copy)
-        acc = acc + recv2[o].astype(F32)
-    send3[...] = acc
-
-    third = [
-        send(send3.at[pl.ds(zz * part, part)], recv3.at[o], 7, o, device(y, zz, core, x))
-        for o, zz in enumerate(zs)
-    ]
-    acc = send3[pl.ds(pl.multiple_of(z * part, part), part)]
-    for o, copy in enumerate(third):
-        copy.wait_recv()
-        acc = acc + recv3[o]
-    tot[...] = acc
+        acc = acc + recv2[o - 1].astype(F32)
+    tot[...] = acc.astype(BF)
 
     place = x * per + lax.rem(z, per)
     fourth = []
@@ -319,7 +330,9 @@
             def _():
                 copy.wait_recv()
 
-    send5[...] = recv4[...].reshape(XN * block, channels).astype(BF)
+    for xx in range(XN):
+        send5[xx * block : (xx + 1) * block, :wide] = recv4[per * xx]
+        send5[xx * block : (xx + 1) * block, wide:] = recv4[per * xx + 1, :, 2 * wide - channels :]
     fifth = send(send5, recv5, 9, 0, sibling)
     rows_n = YN * OWN * GROUP
     cols_n = GROUP * block
@@ -422,11 +435,9 @@
             pltpu.VMEM((GROUP, YN, slots, channels), BF),
             pltpu.VMEM((YN, GROUP, slots, channels), BF),
             pltpu.VMEM((YN, atoms, channels), BF),
-            pltpu.VMEM((YN - 1, atoms, channels), BF),
-            pltpu.VMEM((atoms, channels), F32),
-            pltpu.VMEM((ZN - 1, part, channels), F32),
-            pltpu.VMEM((part, channels), F32),
-            pltpu.VMEM((XN * block // part, part, channels), F32),
+            pltpu.VMEM((YN * ZN - 1, block, 256), BF),
+            pltpu.VMEM((block, 256), BF),
+            pltpu.VMEM((XN * block // part, block, 256), BF),
             pltpu.VMEM((XN * block, channels), BF),
             pltpu.VMEM((XN * block, channels), BF),
             pltpu.VMEM((YN, OWN * GROUP, channels), BF),
@@ -435,6 +446,8 @@
             pltpu.SemaphoreType.DMA((9,)),
             pltpu.SemaphoreType.DMA((11, 8)),
             pltpu.SemaphoreType.DMA((11, 8)),
+            pltpu.SemaphoreType.DMA((YN * ZN - 1,)),
+            pltpu.SemaphoreType.DMA((YN * ZN - 1,)),
         ],
         compiler_params=pltpu.CompilerParams(
             collective_id=0, has_side_effects=True, vmem_limit_bytes=56 << 20

time: 71.6 us -> 74.5 us (1.041)
  Pallas kernels: 70.2 us -> 72.4 us
    pallas_call x1, Pallas kernels: 68.4 us -> 70.6 us  [body(): pl.pallas_call(kernel, out_shape=shapes, in_specs=[HBM] * 9, out_specs=(V...]
where the time goes in v4:
time: 74.5 us; the launch traced here: 73.7 us
  Pallas kernels  72.4 us (97%)
  between operations  1.29 us (2%)
    pallas_call x1, Pallas kernels, body(): pl.pallas_call(kernel, out_shape=shapes, in_specs=[HBM] * 9, out_specs=(V...  70.6 us
    pallas_call x1, Pallas kernels, body(): pl.pallas_call(finish, out_shape=shapes, in_specs=[VMEM] * 2, out_specs=(...  1.79 us

profile of v4, /device:TPU:1, one launch (start us, length us, event | category | flops | bytes accessed | tf_op | source)
XLA Modules:
  0.0 73.7 jit_solution(1713554833458558921)
XLA Ops:
  1.3 70.6 %codes_and_panels.1 = (f32[64,1024]{1,0:T(8,128)}, f32[2,24576]{1,0:T(2,128)}) custom-call(bf16[384,1024]{1,0:T(8,128)(2,1)} %rec_hbm.1, bf16[64,384]{1,0:T(8,128)(2,1)} %maps_hbm.1, f32[64,64]{1,0:T(8,128)} %waves_hbm.1, f32[64,1024]{1,0:T(8,128)} %codes_hbm.1, f32[1,64]{1,0:T(1,128)} %bitcast.5, f32[1,64]{1,0:T(1,128)} %bitcast.6, s32[1,16]{1,0:T(1,128)} %ids_hbm.1, ...), custom_call_target="tpu_custom_call" | custom-call | tf_op jit(solution)/shard_map/codes_and_panels/pallas_call | solution.py:416
  71.9 1.8 %finish.1 = (f32[64,1024]{1,0:T(8,128)}, f32[2,24576]{1,0:T(2,128)}) custom-call(f32[64,1024]{1,0:T(8,128)} %get-tuple-element.4.codes_in, f32[2,24576]{1,0:T(2,128)} %get-tuple-element.5.panels_in), custom_call_target="tpu_custom_call" | custom-call | tf_op jit(solution)/shard_map/finish/pallas_call | solution.py:467

commit v5 on v3

--- a/solution.py
+++ b/solution.py
@@ -29,6 +29,14 @@
 
 def iota(shape, dim):
     return lax.broadcasted_iota(jnp.int32, shape, dim)
+
+
+def over(v, size):
+    return v >> (size.bit_length() - 1)
+
+
+def within(v, size):
+    return v & (size - 1)
 
 
 def to_column(row):
@@ -158,9 +166,9 @@
     half = atoms // 2
     lanes = 8 * half
     pick_lag = iota((64, 8 * lanes), 1)
-    pick_lag = lax.div(pick_lag, lanes) * 8 + lax.div(lax.rem(pick_lag, lanes), half)
+    pick_lag = over(pick_lag, lanes) * 8 + over(within(pick_lag, lanes), half)
     pick_lag = (pick_lag == iota((64, 8 * lanes), 0)).astype(BF)
-    same = (iota((half, lanes), 0) == lax.rem(iota((half, lanes), 1), half)).astype(F32)
+    same = (iota((half, lanes), 0) == within(iota((half, lanes), 1), half)).astype(F32)
     spread = [dot(v, pick_lag) for v in split(waves[...])]
     filters = []
     for g in range(2):
@@ -197,13 +205,8 @@
             groups.append(total)
         return jnp.concatenate(groups, axis=0)
 
-    for copy in halo:
+    for copy in halo[:2]:
         copy.wait_recv()
-    more = [
-        send(rec.at[:, pl.ds(0, 128)], rech, 0, 4, left_id),
-    ]
-    tag_copies = [send(tags, tagr.at[o], 1, o, p) for o, (_, p) in enumerate(pairs)]
-
     first = jnp.where(shard == 0, HALO, 0)
     last = jnp.where(shard == shards - 1, end, width + HALO)
 
@@ -216,14 +219,19 @@
     for (r_from, r_to), (c_from, c_to) in windows:
         synthesis = depthwise(v, 1)[:, r_from - v_from : r_to - v_from]
         high, low = split(synthesis)
-        r = pb[:, r_from:r_to] - dot(gram, jnp.concatenate([high, low, high], axis=0))
+        mixed = dot(gram, jnp.concatenate([high, low, high], axis=0))
+        if v_from == 0:
+            for copy in halo[2:]:
+                copy.wait_recv()
+            more = [send(rec.at[:, pl.ds(0, 128)], rech, 0, 4, left_id)]
+            tag_copies = [send(tags, tagr.at[o], 1, o, p) for o, (_, p) in enumerate(pairs)]
+        r = pb[:, r_from:r_to] - mixed
         r = jnp.where(column(r_from, r_to) < last, r, 0.0)
         g = depthwise(r, -1)[:, c_from - r_from : c_to - r_from]
         v = v[:, c_from - v_from : c_to - v_from]
         v = jnp.maximum(v + step * g - thresh, 0.0)
         v = jnp.where(column(c_from, c_to) < first, 0.0, v)
         v_from = c_from
-    codes_out[...] = v
 
     picked = dot(select, v.astype(BF)).astype(BF)
     picked = jnp.concatenate([picked, jnp.zeros((slots, 128), BF)], axis=1)
@@ -253,10 +261,12 @@
         )
         recv1[rows, me] = chunk[me, rows]
 
+    codes_out[...] = v
+
     for copy in tag_copies:
         copy.wait_recv()
     lane = iota((1, GROUP * slots), 1)
-    source = lax.div(lane, slots)
+    source = over(lane, slots)
     row = jnp.where(source == me, tags[:1], -1.0)
     for o in range(1, GROUP):
         frm = lax.rem(x - o // CN + XN, XN) * CN + lax.rem(core - o % CN + CN, CN)
@@ -330,11 +340,11 @@
     block_owner = jnp.concatenate([block_owner.astype(F32)] * GROUP, axis=1)
     r = iota((rows_n, cols_n), 0)
     c = iota((rows_n, cols_n), 1)
-    wanted_slot = lax.rem(lax.div(r, GROUP), OWN)
-    wanted = ((lax.div(r, OWN * GROUP) * ZN + z) * CN + core) * OWN + wanted_slot
+    wanted_slot = within(over(r, GROUP), OWN)
+    wanted = ((over(r, OWN * GROUP) * ZN + z) * CN + core) * OWN + wanted_slot
     c_core = jnp.where(c < half_n, core, 1 - core)
-    c_group = lax.div(lax.rem(c, half_n), block) * CN + c_core
-    hit = (block_owner == wanted.astype(F32)) & (lax.rem(r, GROUP) == c_group)
+    c_group = over(within(c, half_n), block) * CN + c_core
+    hit = (block_owner == wanted.astype(F32)) & (within(r, GROUP) == c_group)
     hit = hit.astype(BF)
     fifth.wait_recv()
 

time: 71.6 us -> 71.1 us (level)
  no operation moved by 1% of the time
where the time goes in v5:
time: 71.1 us; the launch traced here: 71 us
  Pallas kernels  69.7 us (98%)
  between operations  1.29 us (2%)
    pallas_call x1, Pallas kernels, body(): pl.pallas_call(kernel, out_shape=shapes, in_specs=[HBM] * 9, out_specs=(V...  67.9 us
    pallas_call x1, Pallas kernels, body(): pl.pallas_call(finish, out_shape=shapes, in_specs=[VMEM] * 2, out_specs=(...  1.79 us

profile of v5, /device:TPU:1, one launch (start us, length us, event | category | flops | bytes accessed | tf_op | source)
XLA Modules:
  0.0 71.0 jit_solution(486195110782065652)
XLA Ops:
  1.3 67.9 %codes_and_panels.1 = (f32[64,1024]{1,0:T(8,128)}, f32[2,24576]{1,0:T(2,128)}) custom-call(bf16[384,1024]{1,0:T(8,128)(2,1)} %rec_hbm.1, bf16[64,384]{1,0:T(8,128)(2,1)} %maps_hbm.1, f32[64,64]{1,0:T(8,128)} %waves_hbm.1, f32[64,1024]{1,0:T(8,128)} %codes_hbm.1, f32[1,64]{1,0:T(1,128)} %bitcast.5, f32[1,64]{1,0:T(1,128)} %bitcast.6, s32[1,16]{1,0:T(1,128)} %ids_hbm.1, ...), custom_call_target="tpu_custom_call" | custom-call | tf_op jit(solution)/shard_map/codes_and_panels/pallas_call | solution.py:413
  69.2 1.8 %finish.1 = (f32[64,1024]{1,0:T(8,128)}, f32[2,24576]{1,0:T(2,128)}) custom-call(f32[64,1024]{1,0:T(8,128)} %get-tuple-element.4.codes_in, f32[2,24576]{1,0:T(2,128)} %get-tuple-element.5.panels_in), custom_call_target="tpu_custom_call" | custom-call | tf_op jit(solution)/shard_map/finish/pallas_call | solution.py:464

commit v6 on v5

--- a/solution.py
+++ b/solution.py
@@ -205,6 +205,12 @@
             groups.append(total)
         return jnp.concatenate(groups, axis=0)
 
+    def mix(v):
+        high, low = split(depthwise(v, 1))
+        return dot(gram, jnp.concatenate([high, low, high], axis=0))
+
+    inner_mix = mix(xb[:, HALO:end])
+    inner_back = depthwise(pb[:, HALO:end] - inner_mix, -1)
     for copy in halo[:2]:
         copy.wait_recv()
     first = jnp.where(shard == 0, HALO, 0)
@@ -217,9 +223,13 @@
     v = jnp.where(column(0, width) < first, 0.0, xb[...])
     v_from = 0
     for (r_from, r_to), (c_from, c_to) in windows:
-        synthesis = depthwise(v, 1)[:, r_from - v_from : r_to - v_from]
-        high, low = split(synthesis)
-        mixed = dot(gram, jnp.concatenate([high, low, high], axis=0))
+        if v_from == 0:
+            outer = mix(jnp.concatenate([v[:, :384], v[:, end - 128 :]], axis=1))
+            mixed = jnp.concatenate(
+                [outer[:, 128:384], inner_mix[:, 128:], outer[:, 512:]], axis=1
+            )
+        else:
+            mixed = mix(v)[:, r_from - v_from : r_to - v_from]
         if v_from == 0:
             for copy in halo[2:]:
                 copy.wait_recv()
@@ -227,7 +237,13 @@
             tag_copies = [send(tags, tagr.at[o], 1, o, p) for o, (_, p) in enumerate(pairs)]
         r = pb[:, r_from:r_to] - mixed
         r = jnp.where(column(r_from, r_to) < last, r, 0.0)
-        g = depthwise(r, -1)[:, c_from - r_from : c_to - r_from]
+        if v_from == 0:
+            outer = depthwise(jnp.concatenate([r[:, :384], r[:, end - 256 :]], axis=1), -1)
+            g = jnp.concatenate(
+                [outer[:, :256], inner_back[:, 128 : length - 128], outer[:, 384:640]], axis=1
+            )
+        else:
+            g = depthwise(r, -1)[:, c_from - r_from : c_to - r_from]
         v = v[:, c_from - v_from : c_to - v_from]
         v = jnp.maximum(v + step * g - thresh, 0.0)
         v = jnp.where(column(c_from, c_to) < first, 0.0, v)

time: 71.1 us -> 69.6 us (0.979)
  Pallas kernels: 69.7 us -> 68.2 us
    pallas_call x1, Pallas kernels: 67.9 us -> 66.4 us  [body(): pl.pallas_call(kernel, out_shape=shapes, in_specs=[HBM] * 9, out_specs=(V...]
where the time goes in v6:
time: 69.6 us; the launch traced here: 69.5 us
  Pallas kernels  68.2 us (98%)
  between operations  1.29 us (2%)
    pallas_call x1, Pallas kernels, body(): pl.pallas_call(kernel, out_shape=shapes, in_specs=[HBM] * 9, out_specs=(V...  66.4 us
    pallas_call x1, Pallas kernels, body(): pl.pallas_call(finish, out_shape=shapes, in_specs=[VMEM] * 2, out_specs=(...  1.79 us

profile of v6, /device:TPU:1, one launch (start us, length us, event | category | flops | bytes accessed | tf_op | source)
XLA Modules:
  0.0 69.5 jit_solution(16191099192347253801)
XLA Ops:
  1.3 66.4 %codes_and_panels.1 = (f32[64,1024]{1,0:T(8,128)}, f32[2,24576]{1,0:T(2,128)}) custom-call(bf16[384,1024]{1,0:T(8,128)(2,1)} %rec_hbm.1, bf16[64,384]{1,0:T(8,128)(2,1)} %maps_hbm.1, f32[64,64]{1,0:T(8,128)} %waves_hbm.1, f32[64,1024]{1,0:T(8,128)} %codes_hbm.1, f32[1,64]{1,0:T(1,128)} %bitcast.5, f32[1,64]{1,0:T(1,128)} %bitcast.6, s32[1,16]{1,0:T(1,128)} %ids_hbm.1, ...), custom_call_target="tpu_custom_call" | custom-call | tf_op jit(solution)/shard_map/codes_and_panels/pallas_call | solution.py:429
  67.7 1.8 %finish.1 = (f32[64,1024]{1,0:T(8,128)}, f32[2,24576]{1,0:T(2,128)}) custom-call(f32[64,1024]{1,0:T(8,128)} %get-tuple-element.4.codes_in, f32[2,24576]{1,0:T(2,128)} %get-tuple-element.5.panels_in), custom_call_target="tpu_custom_call" | custom-call | tf_op jit(solution)/shard_map/finish/pallas_call | solution.py:480
